TPU v7x, 128 devices: a whole 4x4x4 slice. The times are simulated.
128 devices in a mesh: dp: 16 (over y, x), mp: 8 (over z, core).
Axes of the slice: x: 4, y: 4, z: 4, core: 2. Of those that a mesh axis runs over, the one named last changes fastest.
Arguments:
- train_in: bfloat16 [128, 256, 11008], P('dp', None, 'mp'), may hold values from -6 to 6
- train_grad_out: bfloat16 [128, 256, 4096], P('dp', None, 'mp'), as said below
- target_in: bfloat16 [128, 256, 11008], P('dp', None, 'mp'), may hold values from -6 to 6
- target_grad_out: bfloat16 [128, 256, 4096], P('dp', None, 'mp'), as said below
- proj_in: bfloat16 [64, 11008], P(None, 'mp'), may hold values from -0.0546875 to 0.0546875
- proj_out: bfloat16 [64, 4096], P(None, 'mp'), may hold values from -0.09375 to 0.09375
Outputs:
- scores: float32 [128, 128], P(('dp', 'mp'))
Inputs may be any that keep to these rules, and one draw needn't show every extreme that they name: `train_grad_out`: every example's output gradients share one positive scale, different from example to example. `target_grad_out`: every example's output gradients share one positive scale, different from example to example.
All inputs are finite; a program needn't handle non-finite values.
Results may differ from a plain program's by a relative error of at most 0.00055.
Values sent between devices are 32-bit elements; how exact they have to be, the bound alone decides.
A program may use at most 128 MiB of HBM per device.

v0:
```python
import jax
import jax.numpy as jnp
from jax import lax
from jax.sharding import PartitionSpec as P

ITERS = 4


def projected_grads(inputs, outputs, proj_in, proj_out, site_pick):
    seq_len = inputs.shape[1]

    def term():
        in_proj = jnp.einsum("etk,rk->etr", inputs, proj_in, preferred_element_type=jnp.float32)
        out_proj = jnp.einsum("etk,rk->etr", outputs, proj_out, preferred_element_type=jnp.float32)
        return jnp.concatenate([out_proj, in_proj], axis=2)

    if site_pick == 0:
        summed = lax.psum_scatter(term(), "mp", scatter_dimension=0, tiled=True)
    else:
        summed = lax.psum_scatter(term(), "mp", scatter_dimension=0, tiled=True)
    rank = proj_in.shape[0]
    out_part = summed[:, :, :rank]
    in_part = summed[:, :, rank:]
    outer = jnp.einsum("eta,etb->eab", out_part, in_part, precision=lax.Precision.HIGHEST)
    return (outer / seq_len).reshape(outer.shape[0], rank * rank)


def local(train_in, train_grad_out, target_in, target_grad_out, proj_in, proj_out):
    train_grads = projected_grads(train_in, train_grad_out, proj_in, proj_out, 0)
    target_local = projected_grads(target_in, target_grad_out, proj_in, proj_out, 1)
    target_grads = lax.all_gather(target_local, ("dp", "mp"), axis=0, tiled=True)
    count = train_grads.shape[0] * lax.axis_size(("dp", "mp"))
    width = train_grads.shape[1]
    trace = lax.psum(jnp.sum(train_grads * train_grads), ("dp", "mp"))
    damping = 0.1 * trace / (count * width)
    solved = jnp.zeros_like(target_grads)
    residual = target_grads
    direction = target_grads
    norm_now = jnp.sum(residual * residual, axis=1, keepdims=True)
    for step in range(ITERS):
        inner = jnp.dot(direction, train_grads.T, precision=lax.Precision.HIGHEST)
        partial_rows = jnp.dot(inner, train_grads, precision=lax.Precision.HIGHEST)
        image = lax.psum(partial_rows, ("dp", "mp")) / count + damping * direction
        alpha = norm_now / jnp.sum(direction * image, axis=1, keepdims=True)
        solved = solved + alpha * direction
        residual = residual - alpha * image
        norm_next = jnp.sum(residual * residual, axis=1, keepdims=True)
        direction = residual + norm_next / norm_now * direction
        norm_now = norm_next
    return jnp.dot(train_grads, solved.T, precision=lax.Precision.HIGHEST)


def solution(mesh):
    return jax.shard_map(
        local,
        mesh=mesh,
        in_specs=(
            P("dp", None, "mp"),
            P("dp", None, "mp"),
            P("dp", None, "mp"),
            P("dp", None, "mp"),
            P(None, "mp"),
            P(None, "mp"),
        ),
        out_specs=P(("dp", "mp"), None),
        check_vma=False,
    )
```

profile of v0, /device:TPU:1, one launch (start us, length us, event | category | flops | bytes accessed | tf_op | source)
XLA Modules:
  0.0 800.0 jit_solution(107940342278195629)
XLA Ops:
  6.5 4.0 fusion.25
  12.4 2.4 fusion.29
  14.8 3.7 fusion.23
  19.7 25.2 %reduce-scatter.5.cloned.1.call-done = f32[1,256,128]{1,2,0:T(8,128)} async-done(((f32[8,256,128]{1,2,0:T(8,128)}), f32[1,256,128]{1,2,0:T(8,128)}) %reduce-scatter.5.cloned.1.call-update) | async-done | bytes 131088 | tf_op jit(solution)/shard_map/reduce_scatter | solution.py:20
  46.7 31.4 %reduce-scatter.3.cloned.1.call-done = f32[1,256,128]{1,2,0:T(8,128)} async-done(((f32[8,256,128]{1,2,0:T(8,128)}), f32[1,256,128]{1,2,0:T(8,128)}) %reduce-scatter.3.cloned.1.call-update) | async-done | bytes 131088 | tf_op jit(solution)/shard_map/reduce_scatter | solution.py:18
  78.1 1.7 multiply_reduce_fusion.6
  79.9 68.8 %all-gather.3.cloned.1.call-done = f32[128,1,4096]{2,1,0:T(1,128)} async-done(((f32[1,1,4096]{2,1,0:T(1,128)}), f32[128,1,4096]{2,1,0:T(1,128)}) %all-gather.3.cloned.1.call-update) | async-done | bytes 2097168 | tf_op jit(solution)/shard_map/all_gather | solution.py:31
  148.7 4.2 fusion.16
  154.6 63.2 %psum.36 = f32[]{:T(128)} all-reduce(f32[]{:T(128)} %get-tuple-element.11), channel_id=1, replica_groups=mesh['dp'=16,'mp'=8] {'dp','mp'}, use_global_device_ids=true, to_apply=%region_5.0 | all-reduce | flops 1 | bytes 8 | tf_op jit(solution)/shard_map/psum | solution.py:34
  218.5 83.6 %all-reduce.5.cloned.1.call-done = f32[128,4096]{1,0:T(8,128)} async-done(((f32[128,4096]{1,0:T(8,128)}), f32[128,4096]{1,0:T(8,128)}) %all-reduce.5.cloned.1.call-update) | async-done | bytes 2097168 | tf_op jit(solution)/shard_map/psum | solution.py:43
  302.1 3.8 fusion.4
  307.3 2.1 fusion.10
  310.7 1.7 convolution_bitcast_fusion.2
  314.2 148.8 %all-reduce.7.cloned.1.call-done = f32[128,4096]{1,0:T(8,128)} async-done(((f32[128,4096]{1,0:T(8,128)}), f32[128,4096]{1,0:T(8,128)}) %all-reduce.7.cloned.1.call-update) | async-done | bytes 2097168 | tf_op jit(solution)/shard_map/psum | solution.py:43
  463.0 2.8 multiply_reduce_fusion.4
  466.4 4.0 multiply_reduce_fusion.3
  473.1 1.7 convolution_bitcast_fusion.1
  476.7 148.6 %all-reduce.9.cloned.1.call-done = f32[128,4096]{1,0:T(8,128)} async-done(((f32[128,4096]{1,0:T(8,128)}), f32[128,4096]{1,0:T(8,128)}) %all-reduce.9.cloned.1.call-update) | async-done | bytes 2097168 | tf_op jit(solution)/shard_map/psum | solution.py:43
  625.2 2.8 multiply_reduce_fusion.2
  628.7 2.2 multiply_reduce_fusion.1
  630.9 1.8 convolution_bitcast_fusion
  634.3 148.8 %all-reduce.11.cloned.1.call-done = f32[128,4096]{1,0:T(8,128)} async-done(((f32[128,4096]{1,0:T(8,128)}), f32[128,4096]{1,0:T(8,128)}) %all-reduce.11.cloned.1.call-update) | async-done | bytes 2097168 | tf_op jit(solution)/shard_map/psum | solution.py:43
  783.2 3.6 multiply_reduce_fusion
  787.9 5.3 fusion.8
  (66 shorter events, 19.6 us)
Async XLA Ops:
  6.5 4.0 copy-start
  6.5 4.0 copy-start.15
  6.5 38.3 %reduce-scatter.5.cloned.1.call-start = ((), (), s32[]{:S(2)}) async-start(), calls=%async_computation.3 | async-start | bytes 1179648 | tf_op jit(solution)/shard_map/reduce_scatter | solution.py:20
  12.4 2.4 copy-start.14
  12.4 65.7 %reduce-scatter.3.cloned.1.call-start = ((), (), s32[]{:S(2)}) async-start(), calls=%async_computation.2 | async-start | bytes 1179648 | tf_op jit(solution)/shard_map/reduce_scatter | solution.py:18
  19.6 129.1 %all-gather.3.cloned.1.call-start = ((), (), s32[]{:S(2)}) async-start(), calls=%async_computation.8 | async-start | bytes 2113536 | tf_op jit(solution)/shard_map/all_gather | solution.py:31
  46.7 255.5 %all-reduce.5.cloned.1.call-start = ((), (), s32[]{:S(2)}) async-start(), calls=%async_computation.4 | async-start | bytes 4194304 | tf_op jit(solution)/shard_map/psum | solution.py:43
  154.5 308.4 %all-reduce.7.cloned.1.call-start = ((), (), s32[]{:S(2)}) async-start(), calls=%async_computation.5 | async-start | bytes 4194304 | tf_op jit(solution)/shard_map/psum | solution.py:43
  302.1 3.8 copy-start.4
  302.1 3.9 copy-start.11
  309.4 1.3 copy-start.7
  314.1 311.1 %all-reduce.9.cloned.1.call-start = ((), (), s32[]{:S(2)}) async-start(), calls=%async_computation.6 | async-start | bytes 4194304 | tf_op jit(solution)/shard_map/psum | solution.py:43
  463.0 2.9 copy-start.5
  463.0 3.5 copy-start.8
  470.4 1.3 copy-start.12
  471.7 1.3 copy-start.1
  476.4 306.8 %all-reduce.11.cloned.1.call-start = ((), (), s32[]{:S(2)}) async-start(), calls=%async_computation.7 | async-start | bytes 4194304 | tf_op jit(solution)/shard_map/psum | solution.py:43
  625.2 2.9 copy-start.2
  625.2 3.5 copy-start.13
  630.9 1.8 copy-start.10
  783.1 3.6 copy-start.3
  783.2 4.1 copy-start.6
  783.2 4.7 copy-start.9
Sparse Core Ops, SparseCore 0:
  12.5 32.3 reduce-scatter.4
  47.3 30.7 reduce-scatter.2
  81.2 67.4 all-gather.2
  154.7 147.4 all-reduce.4
  314.2 148.6 all-reduce.6
  476.5 148.6 all-reduce.8
  634.4 148.6 all-reduce.10
where the time goes:
time: 800 us
  waiting for transfers between devices  655 us (82%)
  blocking collectives  63.2 us (8%)
  other arithmetic  31.4 us (4%)
  matrix products  28.3 us (4%)
  between operations  14.3 us (2%)
    psum x4, waiting for transfers between devices, local(): image = lax.psum(partial_rows, ('dp', 'mp')) / count + damping * direction  530 us
    all_gather x1, waiting for transfers between devices, local(): lax.all_gather(target_local, ('dp', 'mp'), axis=0, tiled=True)  68.8 us
    psum x1, blocking collectives, local(): trace = lax.psum(jnp.sum(train_grads * train_grads), ('dp', 'mp'))  63.2 us
    reduce_scatter x2, waiting for transfers between devices, projected_grads(): summed = lax.psum_scatter(term(), 'mp', scatter_dimension=0, tiled=True)  56.6 us
  transfers between devices with their start and end apart: 7, of which 7 were waited for; matrix products, arithmetic and copies ran while one was open for 1% of the time, Pallas kernels for 0%

commit v1 on v0

v1 whole, which is shorter than its diff:
```python
import functools

import jax
import jax.numpy as jnp
from jax import lax
from jax.experimental import pallas as pl
from jax.experimental.pallas import tpu as pltpu
from jax.sharding import PartitionSpec as P

MESH = pl.DeviceIdType.MESH
F32 = jnp.float32
BF16 = jnp.bfloat16
ITERS = 4
ND, NM, NX, NZ = 16, 8, 4, 4
NDEV = ND * NM
SEQ, LANES, RANK = 256, 128, 64
ROWS = RANK * RANK // LANES
PAIRS = 8
AHEAD = 6
R1, R2, RAW_A, RAW_B, COMB_A, COMB_B = range(6)


def iota(shape, axis):
    return lax.broadcasted_iota(jnp.int32, shape, axis)


def block_row(rows_ref, tile_ref):
    def body(k, acc):
        tiles = [tile_ref[pl.ds(t * 8 * ROWS + k, 8, stride=ROWS), :] for t in range(2)]
        new = []
        for e in range(NM):
            row = rows_ref[pl.ds(e * ROWS + k, 1), :]
            for t in range(2):
                new.append(acc[e * 2 + t] + tiles[t] * row)
        return tuple(new)

    acc = lax.fori_loop(0, ROWS, body, tuple(jnp.zeros((8, LANES), F32) for _ in range(2 * NM)), unroll=4)
    lane, sub = iota((8, LANES), 1), iota((8, LANES), 0)
    spread = jnp.zeros((8, LANES), F32)
    for i in range(2 * NM):
        spread = jnp.where(lane // 8 == i, jnp.sum(acc[i], axis=1, keepdims=True), spread)
    return jnp.sum(jnp.where(lane % 8 == sub, spread, 0.0), axis=0, keepdims=True)


def swap_blocks(tile):
    diag = iota((8, LANES), 1) // 16 == iota((8, LANES), 0)
    out = jnp.where(diag, tile, 0.0)
    for s in range(1, 8):
        moved = jnp.where(diag, pltpu.roll(tile, s * 16, 1), 0.0)
        out = out + pltpu.roll(moved, 8 - s, 0)
    return out


def gradient(out_part, in_part):
    outer = lax.dot_general(
        out_part, in_part, (((1,), (1,)), ((), ())), precision=lax.Precision.HIGHEST, preferred_element_type=F32
    )
    return jnp.concatenate([outer[: RANK // 2, :], outer[RANK // 2 :, :]], axis=1) * (1.0 / SEQ)


def kernel(
    train_in, train_go, target_in, target_go, proj_in, proj_out, out_ref,
    xin, xgo, w_in, w_out, part, sibr, rsr, t_own, b_own, t_m, t_g, b_g, msg, fin, c_mat, k_mat,
    in_sem, w_sem, sib_ss, sib_rs, rs_ss, rs_rs, t_ss, t_rs, b_ss, b_rs, f_ss, f_rs, xsem,
):
    dp, mp = lax.axis_index("dp"), lax.axis_index("mp")
    y, x, z, c = dp // NX, dp % NX, mp // 2, mp % 2
    zp, zm = ((z + 1) % NZ) * 2 + c, ((z + 3) % NZ) * 2 + c

    def item_copies(s, source_in, source_go):
        kidx, mine = (s // 2) % 4, s % 2
        k = (2 + 3 * kidx + 3 * (kidx // 2) + 2 * (kidx // 3)) % 4
        e = ((z + k) % NZ) * 2 + (c + 1 - mine) % 2
        return (
            pltpu.make_async_copy(source_in.at[e], xin.at[s], in_sem.at[s, 0]),
            pltpu.make_async_copy(source_go.at[e], xgo.at[s], in_sem.at[s, 1]),
        )

    def start_item(s):
        @pl.when(s < PAIRS)
        def _():
            for copy in item_copies(s, train_in, train_go):
                copy.start()

        @pl.when((s >= PAIRS) & (s < 2 * PAIRS))
        def _():
            for copy in item_copies(s, target_in, target_go):
                copy.start()

    w_copies = (
        pltpu.make_async_copy(proj_in, w_in, w_sem.at[0]),
        pltpu.make_async_copy(proj_out, w_out, w_sem.at[1]),
    )
    for copy in w_copies:
        copy.start()
    for s in range(AHEAD):
        start_item(s)

    bar = pltpu.get_barrier_semaphore()
    for o in range(1, NM):
        pl.semaphore_signal(bar, inc=1, device_id=(dp, (mp + o) % NM), device_id_type=MESH)
    for o in range(1, 4):
        pl.semaphore_signal(bar, inc=1, device_id=(y * NX + (x + o) % NX, mp), device_id_type=MESH)
        pl.semaphore_signal(bar, inc=1, device_id=(((y + o) % 4) * NX + x, mp), device_id_type=MESH)

    for copy in w_copies:
        copy.wait()

    def project(s):
        for copy in item_copies(s, train_in, train_go):
            copy.wait()
        part[s, :RANK, :] = lax.dot_general(w_out[...], xgo[s], (((1,), (1,)), ((), ())), preferred_element_type=F32)
        part[s, RANK:, :] = jnp.dot(w_in[...], xin[s], preferred_element_type=F32)

    def sib_copy(q):
        return pltpu.make_async_remote_copy(
            src_ref=part.at[2 * q], dst_ref=sibr.at[q], send_sem=sib_ss, recv_sem=sib_rs.at[q],
            device_id=(dp, z * 2 + (1 - c)), device_id_type=MESH,
        )

    def ring_copy(src, ph, slot, to):
        return pltpu.make_async_remote_copy(
            src_ref=src, dst_ref=rsr.at[ph * 6 + slot], send_sem=rs_ss, recv_sem=rs_rs.at[ph * 6 + slot],
            device_id=(dp, to), device_id_type=MESH,
        )

    low, high = pl.ds(0, RANK), pl.ds(RANK, RANK)

    def merge(q):
        sib_copy(q).wait_recv()
        s, ph, kidx = 2 * q + 1, q // 4, q % 4
        part[s] = part[s] + sibr[q]

        @pl.when(kidx == 0)
        def _():
            ring_copy(part.at[s, low], ph, R1, zp).start()
            ring_copy(part.at[s, high], ph, R2, zm).start()

        @pl.when(kidx == 1)
        def _():
            ring_copy(part.at[s, high], ph, RAW_B, zp).start()

        @pl.when(kidx == 2)
        def _():
            ring_copy(part.at[s, low], ph, RAW_A, zm).start()

    project(0)
    project(1)
    pl.semaphore_wait(bar, NM - 1 + 6)
    sib_copy(0).start()
    for o in range(1, 4):
        pl.semaphore_signal(xsem, inc=1, device_id=(y * NX + (x + o) % NX, mp), device_id_type=MESH)
    start_item(AHEAD)
    start_item(AHEAD + 1)

    def pair(q, carry):
        project(2 * q)
        sib_copy(q).start()
        project(2 * q + 1)
        start_item(2 * q + AHEAD)
        start_item(2 * q + 1 + AHEAD)
        merge(q - 1)
        return carry

    lax.fori_loop(1, PAIRS, pair, 0)
    merge(PAIRS - 1)

    def forward(ph):
        s_next, s_prev = 2 * (4 * ph + 1) + 1, 2 * (4 * ph + 2) + 1
        ring_copy(part.at[s_next, low], ph, R1, zp).wait_recv()
        part[s_next, :RANK, :] = part[s_next, :RANK, :] + rsr[ph * 6 + R1]
        ring_copy(part.at[s_next, low], ph, COMB_A, zp).start()
        ring_copy(part.at[s_prev, high], ph, R2, zm).wait_recv()
        part[s_prev, RANK:, :] = part[s_prev, RANK:, :] + rsr[ph * 6 + R2]
        ring_copy(part.at[s_prev, high], ph, COMB_B, zm).start()

    def finish(ph):
        s = 2 * (4 * ph + 3) + 1
        for slot in (RAW_A, RAW_B, COMB_A, COMB_B):
            ring_copy(part.at[s, low], ph, slot, zp).wait_recv()
        top = part[s, :RANK, :] + rsr[ph * 6 + RAW_A] + rsr[ph * 6 + COMB_A]
        bottom = part[s, RANK:, :] + rsr[ph * 6 + RAW_B] + rsr[ph * 6 + COMB_B]
        return gradient(top, bottom)

    forward(0)
    forward(1)

    own_d, own_m = pl.ds(pl.multiple_of(dp * ROWS, ROWS), ROWS), pl.ds(pl.multiple_of(mp * ROWS, ROWS), ROWS)

    def mp_copy(o, src, dst, ss, rs):
        return pltpu.make_async_remote_copy(
            src_ref=src, dst_ref=dst.at[own_m], send_sem=ss, recv_sem=rs, device_id=(dp, (mp + o) % NM), device_id_type=MESH
        )

    def dp_copy(o, src, dst, ss, rs):
        return pltpu.make_async_remote_copy(
            src_ref=src, dst_ref=dst.at[own_d], send_sem=ss, recv_sem=rs, device_id=((dp + o) % ND, mp), device_id_type=MESH
        )

    train_row = finish(0)
    t_own[...] = train_row
    pl.semaphore_wait(xsem, 3)
    for o in range(1, ND):
        dp_copy(o, t_own, t_m, t_ss.at[0], t_rs.at[0]).start()
    for o in range(1, NM):
        mp_copy(o, t_own, t_g, t_ss.at[1], t_rs.at[1]).start()
    t_m[own_d, :] = train_row
    t_g[own_m, :] = train_row

    target_row = finish(1)
    b_own[...] = target_row
    for o in range(1, NM):
        mp_copy(o, b_own, b_g, b_ss, b_rs).start()
    b_g[own_m, :] = target_row
    msg[2:3, :] = jnp.broadcast_to(jnp.sum(target_row * target_row), (1, LANES))
    msg[3:4, :] = jnp.zeros((1, LANES), F32)

    def bytes_of(ref, sem):
        return pltpu.make_async_copy(ref, ref, sem)

    dp_rest, mp_rest = pl.ds(0, (ND - 1) * ROWS), pl.ds(0, (NM - 1) * ROWS)
    bytes_of(t_m.at[dp_rest], t_rs.at[0]).wait()
    bytes_of(t_g.at[mp_rest], t_rs.at[1]).wait()
    msg[1:2, :] = block_row(t_g, t_m)
    bytes_of(b_g.at[mp_rest], b_rs).wait()
    msg[0:1, :] = block_row(b_g, t_m)

    me = dp * NM + mp

    def send_all(o, carry):
        to_y, to_x = (y + 2 + o // 32) % 4, (x + 2 + (o // 8) % 4) % 4
        to_z, to_c = (z + 2 + (o // 2) % 4) % 4, (c + 1 + o) % 2
        to_dp, to_mp = to_y * NX + to_x, to_z * 2 + to_c

        @pl.when(to_dp * NM + to_mp != me)
        def _():
            pltpu.make_async_remote_copy(
                src_ref=msg, dst_ref=fin.at[me], send_sem=f_ss, recv_sem=f_rs, device_id=(to_dp, to_mp), device_id_type=MESH
            ).start()

        return carry

    lax.fori_loop(0, NDEV, send_all, 0)
    fin[me] = msg[...]
    bytes_of(fin.at[pl.ds(0, NDEV - 1)], f_rs).wait()

    for d in range(ND):
        rows = pl.ds(d * NM, NM)
        c_mat[rows, :] = swap_blocks(fin[rows, 0, :])
        k_mat[pl.ds(d, NM, stride=ND), :] = swap_blocks(fin[rows, 1, :])
    norm = fin[:, 2, :][:, :1]

    gram = k_mat[...]
    lane, sub = iota((NDEV, LANES), 1), iota((NDEV, LANES), 0)
    trace = jnp.sum(jnp.where(lane == sub, gram, 0.0), keepdims=True)
    damping = trace * (0.1 / (NDEV * RANK * RANK))
    inv = 1.0 / NDEV
    u_res = c_mat[...]
    u_dir, scores, dir_norm = u_res, jnp.zeros_like(u_res), norm
    for step in range(ITERS):
        u_norm = jnp.sum(u_dir * u_dir, axis=1, keepdims=True)
        alpha = norm / (damping * dir_norm + u_norm * inv)
        scores = scores + alpha * u_dir
        if step == ITERS - 1:
            break
        image = lax.dot_general(u_dir, gram, (((1,), (0,)), ((), ())), precision=lax.Precision.HIGHEST, preferred_element_type=F32)
        u_gram = jnp.sum(u_dir * image, axis=1, keepdims=True)
        squared = damping * damping * dir_norm + 2.0 * inv * damping * u_norm + inv * inv * u_gram
        following = alpha * alpha * squared - norm
        u_res = u_res - alpha * (damping * u_dir + inv * image)
        ratio = following / norm
        u_dir = u_res + ratio * u_dir
        dir_norm = following + ratio * ratio * dir_norm
        norm = following
    column = jnp.sum(jnp.where(lane == mp * ND + dp, scores, 0.0), axis=1, keepdims=True)
    out_ref[...] = jnp.sum(jnp.where(lane == sub, column, 0.0), axis=0, keepdims=True)

    bytes_of(part.at[pl.ds(0, PAIRS)], sib_ss).wait()
    bytes_of(rsr, rs_ss).wait()
    bytes_of(t_m.at[dp_rest], t_ss.at[0]).wait()
    bytes_of(t_g.at[mp_rest], t_ss.at[1]).wait()
    bytes_of(b_g.at[mp_rest], b_ss).wait()
    bytes_of(fin.at[pl.ds(0, NDEV - 1)], f_ss).wait()


def local(train_in, train_grad_out, target_in, target_grad_out, proj_in, proj_out):
    d_in, d_out = proj_in.shape[1], proj_out.shape[1]
    dma, vmem = pltpu.SemaphoreType.DMA, pltpu.VMEM
    return pl.pallas_call(
        kernel,
        out_shape=jax.ShapeDtypeStruct((1, NDEV), F32),
        in_specs=[pl.BlockSpec(memory_space=pltpu.HBM)] * 6,
        out_specs=pl.BlockSpec(memory_space=pltpu.VMEM),
        scratch_shapes=[
            vmem((2 * PAIRS, d_in, SEQ), BF16),
            vmem((2 * PAIRS, SEQ, d_out), BF16),
            vmem((RANK, d_in), BF16),
            vmem((RANK, d_out), BF16),
            vmem((2 * PAIRS, 2 * RANK, SEQ), F32),
            vmem((PAIRS, 2 * RANK, SEQ), F32),
            vmem((12, RANK, SEQ), F32),
            vmem((ROWS, LANES), F32),
            vmem((ROWS, LANES), F32),
            vmem((ND * ROWS, LANES), F32),
            vmem((NM * ROWS, LANES), F32),
            vmem((NM * ROWS, LANES), F32),
            vmem((4, LANES), F32),
            vmem((NDEV, 4, LANES), F32),
            vmem((NDEV, LANES), F32),
            vmem((NDEV, LANES), F32),
            dma((2 * PAIRS, 2)),
            dma((2,)),
            dma,
            dma((PAIRS,)),
            dma,
            dma((12,)),
            dma((2,)),
            dma((2,)),
            dma,
            dma,
            dma,
            dma,
            pltpu.SemaphoreType.REGULAR,
        ],
        compiler_params=pltpu.CompilerParams(collective_id=0, has_side_effects=True, vmem_limit_bytes=60 * 1024 * 1024),
    )(train_in.swapaxes(1, 2), train_grad_out, target_in.swapaxes(1, 2), target_grad_out, proj_in, proj_out)


def solution(mesh):
    return jax.shard_map(
        local,
        mesh=mesh,
        in_specs=(
            P("dp", None, "mp"),
            P("dp", None, "mp"),
            P("dp", None, "mp"),
            P("dp", None, "mp"),
            P(None, "mp"),
            P(None, "mp"),
        ),
        out_specs=P(("dp", "mp"), None),
        check_vma=False,
    )
```

time: 800 us -> 40.8 us (0.05)
  waiting for transfers between devices: 655 us -> 0 us
  blocking collectives: 63.2 us -> 0 us
  Pallas kernels: 0 us -> 39.5 us
  other arithmetic: 31.4 us -> 0 us
  matrix products: 28.3 us -> 0 us
  between operations: 14.3 us -> 0.01 us
    psum x4 -> x0, waiting for transfers between devices: 530 us -> none  [local(): image = lax.psum(partial_rows, ('dp', 'mp')) / count + damping * direction]
    all_gather x1 -> x0, waiting for transfers between devices: 68.8 us -> none  [local(): lax.all_gather(target_local, ('dp', 'mp'), axis=0, tiled=True)]
    psum x1 -> x0, blocking collectives: 63.2 us -> none  [local(): trace = lax.psum(jnp.sum(train_grads * train_grads), ('dp', 'mp'))]
    reduce_scatter x2 -> x0, waiting for transfers between devices: 56.6 us -> none  [projected_grads(): summed = lax.psum_scatter(term(), 'mp', scatter_dimension=0, tiled=True)]
    pallas_call x0 -> x1, Pallas kernels: none -> 39.5 us  [local(): pl.pallas_call(kernel, out_shape=jax.ShapeDtypeStruct((1, NDEV), F32), in...]
    dot_general x11 -> x0, matrix products: 28.3 us -> none  [the longest x4 9.48 us: local(): inner = jnp.dot(direction, train_grads.T, precision=lax.Precision.HIGHEST)]
    reduce_sum x7 -> x0, other arithmetic: 20.5 us -> none  [the longest x4 13 us: local(): alpha = norm_now / jnp.sum(direction * image, axis=1, keepdims=True)]
  transfers between devices with their start and end apart: 7 -> 0, of which waited for: 7 -> 0; matrix products, arithmetic and copies ran while one was open for 1% -> 0% of each run, Pallas kernels for 0% -> 0%
where the time goes in v1:
time: 40.8 us; the launch traced here: 40.7 us
  Pallas kernels  39.5 us (97%)
  local copies, waits for them, and re-layouts  1.19 us (3%)
    pallas_call x1, Pallas kernels, local(): pl.pallas_call(kernel, out_shape=jax.ShapeDtypeStruct((1, NDEV), F32), in...  39.5 us
    unnamed x1, local copies, waits for them, and re-layouts  1.19 us

profile of v1, /device:TPU:1, one launch (start us, length us, event | category | flops | bytes accessed | tf_op | source)
XLA Modules:
  0.0 40.7 jit_solution(8903340555409122214)
XLA Ops:
  0.0 39.5 %shard_map.64 = f32[1,128]{1,0:T(1,128)} custom-call(bf16[8,1376,256]{2,1,0:T(8,128)(2,1)} %bitcast.2, bf16[8,256,512]{2,1,0:T(8,128)(2,1)} %train_go.1, bf16[8,1376,256]{2,1,0:T(8,128)(2,1)} %bitcast.3, bf16[8,256,512]{2,1,0:T(8,128)(2,1)} %target_go.1, bf16[64,1376]{1,0:T(8,128)(2,1)} %proj_in.1, bf16[64,512]{1,0:T(8,128)(2,1)} %proj_out.1), custom_call_target="tpu_custom_call" | custom-call | tf_op jit(solution)/shard_map/pallas_call | solution.py:289
  39.5 1.2 %copy.8 = f32[1,128]{1,0:T(1,128)} copy(f32[1,128]{1,0:T(1,128)} %shard_map.64) | data formatting | bytes 1024

commit v2 on v1

--- a/solution.py
+++ b/solution.py
@@ -17,6 +17,11 @@
 ROWS = RANK * RANK // LANES
 PAIRS = 8
 AHEAD = 6
+LAG = 2
+FORWARD_AT = 6
+ORDER = ((0, 2), (1, 2), (0, 1), (0, 3), (1, 1), (1, 3), (0, 0), (1, 0))
+PHASE_BITS = sum(ph << q for q, (ph, _) in enumerate(ORDER))
+CHIP_BITS = sum(k << 2 * q for q, (_, k) in enumerate(ORDER))
 R1, R2, RAW_A, RAW_B, COMB_A, COMB_B = range(6)
 
 
@@ -68,21 +73,22 @@
     zp, zm = ((z + 1) % NZ) * 2 + c, ((z + 3) % NZ) * 2 + c
 
     def item_copies(s, source_in, source_go):
-        kidx, mine = (s // 2) % 4, s % 2
-        k = (2 + 3 * kidx + 3 * (kidx // 2) + 2 * (kidx // 3)) % 4
-        e = ((z + k) % NZ) * 2 + (c + 1 - mine) % 2
+        k = lax.shift_right_logical(CHIP_BITS, 2 * (s // 2)) & 3
+        e = ((z + k) % NZ) * 2 + (c + 1 + s) % 2
         return (
             pltpu.make_async_copy(source_in.at[e], xin.at[s], in_sem.at[s, 0]),
             pltpu.make_async_copy(source_go.at[e], xgo.at[s], in_sem.at[s, 1]),
         )
 
     def start_item(s):
-        @pl.when(s < PAIRS)
+        phase = lax.shift_right_logical(PHASE_BITS, s // 2) & 1
+
+        @pl.when((phase == 0) & (s < 2 * PAIRS))
         def _():
             for copy in item_copies(s, train_in, train_go):
                 copy.start()
 
-        @pl.when((s >= PAIRS) & (s < 2 * PAIRS))
+        @pl.when((phase == 1) & (s < 2 * PAIRS))
         def _():
             for copy in item_copies(s, target_in, target_go):
                 copy.start()
@@ -93,7 +99,7 @@
     )
     for copy in w_copies:
         copy.start()
-    for s in range(AHEAD):
+    for s in range(2):
         start_item(s)
 
     bar = pltpu.get_barrier_semaphore()
@@ -105,6 +111,8 @@
 
     for copy in w_copies:
         copy.wait()
+    for s in range(2, AHEAD):
+        start_item(s)
 
     def project(s):
         for copy in item_copies(s, train_in, train_go):
@@ -128,21 +136,39 @@
 
     def merge(q):
         sib_copy(q).wait_recv()
-        s, ph, kidx = 2 * q + 1, q // 4, q % 4
+        s = 2 * q + 1
         part[s] = part[s] + sibr[q]
-
-        @pl.when(kidx == 0)
-        def _():
-            ring_copy(part.at[s, low], ph, R1, zp).start()
-            ring_copy(part.at[s, high], ph, R2, zm).start()
-
-        @pl.when(kidx == 1)
-        def _():
-            ring_copy(part.at[s, high], ph, RAW_B, zp).start()
-
-        @pl.when(kidx == 2)
-        def _():
-            ring_copy(part.at[s, low], ph, RAW_A, zm).start()
+        for j, (ph, k) in enumerate(ORDER):
+
+            @pl.when(q == j)
+            def _():
+                if k == 2:
+                    ring_copy(part.at[s, low], ph, R1, zp).start()
+                    ring_copy(part.at[s, high], ph, R2, zm).start()
+                if k == 1:
+                    ring_copy(part.at[s, high], ph, RAW_B, zp).start()
+                if k == 3:
+                    ring_copy(part.at[s, low], ph, RAW_A, zm).start()
+
+    def slot_of(ph, k):
+        return 2 * ORDER.index((ph, k)) + 1
+
+    def forward(ph):
+        s_next, s_prev = slot_of(ph, 1), slot_of(ph, 3)
+        ring_copy(part.at[s_next, low], ph, R1, zp).wait_recv()
+        part[s_next, :RANK, :] = part[s_next, :RANK, :] + rsr[ph * 6 + R1]
+        ring_copy(part.at[s_next, low], ph, COMB_A, zp).start()
+        ring_copy(part.at[s_prev, high], ph, R2, zm).wait_recv()
+        part[s_prev, RANK:, :] = part[s_prev, RANK:, :] + rsr[ph * 6 + R2]
+        ring_copy(part.at[s_prev, high], ph, COMB_B, zm).start()
+
+    def finish(ph):
+        s = slot_of(ph, 0)
+        for slot in (RAW_A, RAW_B, COMB_A, COMB_B):
+            ring_copy(part.at[s, low], ph, slot, zp).wait_recv()
+        top = part[s, :RANK, :] + rsr[ph * 6 + RAW_A] + rsr[ph * 6 + COMB_A]
+        bottom = part[s, RANK:, :] + rsr[ph * 6 + RAW_B] + rsr[ph * 6 + COMB_B]
+        return gradient(top, bottom)
 
     project(0)
     project(1)
@@ -159,30 +185,19 @@
         project(2 * q + 1)
         start_item(2 * q + AHEAD)
         start_item(2 * q + 1 + AHEAD)
-        merge(q - 1)
+        @pl.when(q >= LAG)
+        def _():
+            merge(q - LAG)
+
+        @pl.when(q == FORWARD_AT)
+        def _():
+            forward(0)
+
         return carry
 
     lax.fori_loop(1, PAIRS, pair, 0)
-    merge(PAIRS - 1)
-
-    def forward(ph):
-        s_next, s_prev = 2 * (4 * ph + 1) + 1, 2 * (4 * ph + 2) + 1
-        ring_copy(part.at[s_next, low], ph, R1, zp).wait_recv()
-        part[s_next, :RANK, :] = part[s_next, :RANK, :] + rsr[ph * 6 + R1]
-        ring_copy(part.at[s_next, low], ph, COMB_A, zp).start()
-        ring_copy(part.at[s_prev, high], ph, R2, zm).wait_recv()
-        part[s_prev, RANK:, :] = part[s_prev, RANK:, :] + rsr[ph * 6 + R2]
-        ring_copy(part.at[s_prev, high], ph, COMB_B, zm).start()
-
-    def finish(ph):
-        s = 2 * (4 * ph + 3) + 1
-        for slot in (RAW_A, RAW_B, COMB_A, COMB_B):
-            ring_copy(part.at[s, low], ph, slot, zp).wait_recv()
-        top = part[s, :RANK, :] + rsr[ph * 6 + RAW_A] + rsr[ph * 6 + COMB_A]
-        bottom = part[s, RANK:, :] + rsr[ph * 6 + RAW_B] + rsr[ph * 6 + COMB_B]
-        return gradient(top, bottom)
-
-    forward(0)
+    for q in range(PAIRS - LAG, PAIRS):
+        merge(q)
     forward(1)
 
     own_d, own_m = pl.ds(pl.multiple_of(dp * ROWS, ROWS), ROWS), pl.ds(pl.multiple_of(mp * ROWS, ROWS), ROWS)
@@ -213,7 +228,6 @@
         mp_copy(o, b_own, b_g, b_ss, b_rs).start()
     b_g[own_m, :] = target_row
     msg[2:3, :] = jnp.broadcast_to(jnp.sum(target_row * target_row), (1, LANES))
-    msg[3:4, :] = jnp.zeros((1, LANES), F32)
 
     def bytes_of(ref, sem):
         return pltpu.make_async_copy(ref, ref, sem)
@@ -227,20 +241,12 @@
 
     me = dp * NM + mp
 
-    def send_all(o, carry):
-        to_y, to_x = (y + 2 + o // 32) % 4, (x + 2 + (o // 8) % 4) % 4
-        to_z, to_c = (z + 2 + (o // 2) % 4) % 4, (c + 1 + o) % 2
-        to_dp, to_mp = to_y * NX + to_x, to_z * 2 + to_c
-
-        @pl.when(to_dp * NM + to_mp != me)
-        def _():
-            pltpu.make_async_remote_copy(
-                src_ref=msg, dst_ref=fin.at[me], send_sem=f_ss, recv_sem=f_rs, device_id=(to_dp, to_mp), device_id_type=MESH
-            ).start()
-
-        return carry
-
-    lax.fori_loop(0, NDEV, send_all, 0)
+    to_dps = [((y + dy) % 4) * NX + (x + dx) % NX for dy in (2, 1, 3, 0) for dx in (2, 1, 3, 0)]
+    to_mps = [((z + dz) % NZ) * 2 + (c + dc) % 2 for dz in (2, 1, 3, 0) for dc in (1, 0)]
+    for to in [(to_dp, to_mp) for to_dp in to_dps for to_mp in to_mps][:-1]:
+        pltpu.make_async_remote_copy(
+            src_ref=msg, dst_ref=fin.at[me], send_sem=f_ss, recv_sem=f_rs, device_id=to, device_id_type=MESH
+        ).start()
     fin[me] = msg[...]
     bytes_of(fin.at[pl.ds(0, NDEV - 1)], f_rs).wait()
 
@@ -273,7 +279,8 @@
         dir_norm = following + ratio * ratio * dir_norm
         norm = following
     column = jnp.sum(jnp.where(lane == mp * ND + dp, scores, 0.0), axis=1, keepdims=True)
-    out_ref[...] = jnp.sum(jnp.where(lane == sub, column, 0.0), axis=0, keepdims=True)
+    spread = jnp.where(lane == sub, column, 0.0)
+    out_ref[...] = sum(spread[8 * d : 8 * d + 8, :] for d in range(ND))
 
     bytes_of(part.at[pl.ds(0, PAIRS)], sib_ss).wait()
     bytes_of(rsr, rs_ss).wait()
@@ -286,9 +293,9 @@
 def local(train_in, train_grad_out, target_in, target_grad_out, proj_in, proj_out):
     d_in, d_out = proj_in.shape[1], proj_out.shape[1]
     dma, vmem = pltpu.SemaphoreType.DMA, pltpu.VMEM
-    return pl.pallas_call(
+    spread = pl.pallas_call(
         kernel,
-        out_shape=jax.ShapeDtypeStruct((1, NDEV), F32),
+        out_shape=jax.ShapeDtypeStruct((8, NDEV), F32),
         in_specs=[pl.BlockSpec(memory_space=pltpu.HBM)] * 6,
         out_specs=pl.BlockSpec(memory_space=pltpu.VMEM),
         scratch_shapes=[
@@ -304,8 +311,8 @@
             vmem((ND * ROWS, LANES), F32),
             vmem((NM * ROWS, LANES), F32),
             vmem((NM * ROWS, LANES), F32),
-            vmem((4, LANES), F32),
-            vmem((NDEV, 4, LANES), F32),
+            vmem((3, LANES), F32),
+            vmem((NDEV, 3, LANES), F32),
             vmem((NDEV, LANES), F32),
             vmem((NDEV, LANES), F32),
             dma((2 * PAIRS, 2)),
@@ -322,8 +329,12 @@
             dma,
             pltpu.SemaphoreType.REGULAR,
         ],
-        compiler_params=pltpu.CompilerParams(collective_id=0, has_side_effects=True, vmem_limit_bytes=60 * 1024 * 1024),
-    )(train_in.swapaxes(1, 2), train_grad_out, target_in.swapaxes(1, 2), target_grad_out, proj_in, proj_out)
+        compiler_params=pltpu.CompilerParams(collective_id=0, has_side_effects=True, vmem_limit_bytes=32 * 1024 * 1024),
+    )(*(
+        pltpu.with_memory_space_constraint(a, pltpu.HBM)
+        for a in (train_in.swapaxes(1, 2), train_grad_out, target_in.swapaxes(1, 2), target_grad_out, proj_in, proj_out)
+    ))
+    return jnp.sum(spread, axis=0, keepdims=True)
 
 
 def solution(mesh):

time: 40.8 us -> 34.7 us (0.85)
  Pallas kernels: 39.5 us -> 34 us
  local copies, waits for them, and re-layouts: 1.19 us -> 0 us
  other arithmetic: 0 us -> 0.53 us
    pallas_call x1, Pallas kernels: 39.5 us -> 34 us  [local(): pl.pallas_call(kernel, out_shape=jax.ShapeDtypeStruct((8, NDEV), F32), in...]
    unnamed x1 -> x0, local copies, waits for them, and re-layouts: 1.19 us -> none
    reduce_sum x0 -> x1, other arithmetic: none -> 0.53 us  [local(): return jnp.sum(spread, axis=0, keepdims=True)]
where the time goes in v2:
time: 34.7 us; the launch traced here: 34.6 us
  Pallas kernels  34 us (98%)
  other arithmetic  0.53 us (2%)
    pallas_call x1, Pallas kernels, local(): pl.pallas_call(kernel, out_shape=jax.ShapeDtypeStruct((8, NDEV), F32), in...  34 us

profile of v2, /device:TPU:1, one launch (start us, length us, event | category | flops | bytes accessed | tf_op | source)
XLA Modules:
  0.0 34.6 jit_solution(4058710422162499470)
XLA Ops:
  0.0 34.0 %shard_map.64 = f32[8,128]{1,0:T(8,128)S(1)} custom-call(bf16[8,1376,256]{2,1,0:T(8,128)(2,1)} %bitcast.3, bf16[8,256,512]{2,1,0:T(8,128)(2,1)} %train_go.1, bf16[8,1376,256]{2,1,0:T(8,128)(2,1)} %bitcast.4, bf16[8,256,512]{2,1,0:T(8,128)(2,1)} %target_go.1, bf16[64,1376]{1,0:T(8,128)(2,1)} %proj_in.1, bf16[64,512]{1,0:T(8,128)(2,1)} %proj_out.1), custom_call_target="tpu_custom_call" | custom-call | tf_op jit(solution)/shard_map/pallas_call | solution.py:296
  34.1 0.5 %reduce_sum.9 = f32[128]{0:T(128)} reduce(f32[8,128]{1,0:T(8,128)S(1)} %shard_map.64, f32[]{:T(128)} %constant.0.clone.1), dimensions={0}, to_apply=%region_0.0 | reduce | flops 896 | bytes 4612 | tf_op jit(solution)/shard_map/reduce_sum | solution.py:337

commit v3 on v2

--- a/solution.py
+++ b/solution.py
@@ -18,7 +18,7 @@
 PAIRS = 8
 AHEAD = 6
 LAG = 2
-FORWARD_AT = 6
+FORWARD_AT = 5
 ORDER = ((0, 2), (1, 2), (0, 1), (0, 3), (1, 1), (1, 3), (0, 0), (1, 0))
 PHASE_BITS = sum(ph << q for q, (ph, _) in enumerate(ORDER))
 CHIP_BITS = sum(k << 2 * q for q, (_, k) in enumerate(ORDER))
@@ -93,14 +93,14 @@
             for copy in item_copies(s, target_in, target_go):
                 copy.start()
 
-    w_copies = (
-        pltpu.make_async_copy(proj_in, w_in, w_sem.at[0]),
-        pltpu.make_async_copy(proj_out, w_out, w_sem.at[1]),
-    )
-    for copy in w_copies:
-        copy.start()
-    for s in range(2):
-        start_item(s)
+    w_copies = (pltpu.make_async_copy(proj_out, w_out, w_sem.at[0]), pltpu.make_async_copy(proj_in, w_in, w_sem.at[1]))
+    first = [item_copies(s, train_in, train_go) for s in range(2)]
+    w_copies[0].start()
+    for copies in first:
+        copies[1].start()
+    w_copies[1].start()
+    for copies in first:
+        copies[0].start()
 
     bar = pltpu.get_barrier_semaphore()
     for o in range(1, NM):
@@ -109,10 +109,13 @@
         pl.semaphore_signal(bar, inc=1, device_id=(y * NX + (x + o) % NX, mp), device_id_type=MESH)
         pl.semaphore_signal(bar, inc=1, device_id=(((y + o) % 4) * NX + x, mp), device_id_type=MESH)
 
-    for copy in w_copies:
-        copy.wait()
-    for s in range(2, AHEAD):
-        start_item(s)
+    def project_out(s):
+        item_copies(s, train_in, train_go)[1].wait()
+        part[s, :RANK, :] = lax.dot_general(w_out[...], xgo[s], (((1,), (1,)), ((), ())), preferred_element_type=F32)
+
+    def project_in(s):
+        item_copies(s, train_in, train_go)[0].wait()
+        part[s, RANK:, :] = jnp.dot(w_in[...], xin[s], preferred_element_type=F32)
 
     def project(s):
         for copy in item_copies(s, train_in, train_go):
@@ -120,6 +123,22 @@
         part[s, :RANK, :] = lax.dot_general(w_out[...], xgo[s], (((1,), (1,)), ((), ())), preferred_element_type=F32)
         part[s, RANK:, :] = jnp.dot(w_in[...], xin[s], preferred_element_type=F32)
 
+    low, high = pl.ds(0, RANK), pl.ds(RANK, RANK)
+
+    def sib_half(half, sem):
+        return pltpu.make_async_remote_copy(
+            src_ref=part.at[0, half], dst_ref=sibr.at[0, half], send_sem=sib_ss, recv_sem=sib_rs.at[sem],
+            device_id=(dp, z * 2 + (1 - c)), device_id_type=MESH,
+        )
+
+    def project_pair(q):
+        for s in (2 * q, 2 * q + 1):
+            for copy in item_copies(s, train_in, train_go):
+                copy.wait()
+        for s in (2 * q, 2 * q + 1):
+            part[s, :RANK, :] = lax.dot_general(w_out[...], xgo[s], (((1,), (1,)), ((), ())), preferred_element_type=F32)
+            part[s, RANK:, :] = jnp.dot(w_in[...], xin[s], preferred_element_type=F32)
+
     def sib_copy(q):
         return pltpu.make_async_remote_copy(
             src_ref=part.at[2 * q], dst_ref=sibr.at[q], send_sem=sib_ss, recv_sem=sib_rs.at[q],
@@ -131,14 +150,12 @@
             src_ref=src, dst_ref=rsr.at[ph * 6 + slot], send_sem=rs_ss, recv_sem=rs_rs.at[ph * 6 + slot],
             device_id=(dp, to), device_id_type=MESH,
         )
-
-    low, high = pl.ds(0, RANK), pl.ds(RANK, RANK)
 
     def merge(q):
         sib_copy(q).wait_recv()
         s = 2 * q + 1
         part[s] = part[s] + sibr[q]
-        for j, (ph, k) in enumerate(ORDER):
+        for j, (ph, k) in list(enumerate(ORDER))[1:]:
 
             @pl.when(q == j)
             def _():
@@ -170,22 +187,37 @@
         bottom = part[s, RANK:, :] + rsr[ph * 6 + RAW_B] + rsr[ph * 6 + COMB_B]
         return gradient(top, bottom)
 
-    project(0)
-    project(1)
+    w_copies[0].wait()
+    project_out(0)
+    project_out(1)
+    for s in range(2, AHEAD):
+        start_item(s)
     pl.semaphore_wait(bar, NM - 1 + 6)
-    sib_copy(0).start()
+    sib_half(low, 0).start()
     for o in range(1, 4):
         pl.semaphore_signal(xsem, inc=1, device_id=(y * NX + (x + o) % NX, mp), device_id_type=MESH)
-    start_item(AHEAD)
-    start_item(AHEAD + 1)
+    w_copies[1].wait()
+    project_in(0)
+    sib_half(high, PAIRS).start()
+    project_in(1)
+    for s in range(AHEAD, AHEAD + 2):
+        start_item(s)
+    sib_half(low, 0).wait_recv()
+    part[1, :RANK, :] = part[1, :RANK, :] + sibr[0, :RANK, :]
+    ring_copy(part.at[1, low], 0, R1, zp).start()
 
     def pair(q, carry):
-        project(2 * q)
+        project_pair(q)
         sib_copy(q).start()
-        project(2 * q + 1)
         start_item(2 * q + AHEAD)
         start_item(2 * q + 1 + AHEAD)
-        @pl.when(q >= LAG)
+        @pl.when(q == 1)
+        def _():
+            sib_half(high, PAIRS).wait_recv()
+            part[1, RANK:, :] = part[1, RANK:, :] + sibr[0, RANK:, :]
+            ring_copy(part.at[1, high], 0, R2, zm).start()
+
+        @pl.when(q > LAG)
         def _():
             merge(q - LAG)
 
@@ -227,7 +259,7 @@
     for o in range(1, NM):
         mp_copy(o, b_own, b_g, b_ss, b_rs).start()
     b_g[own_m, :] = target_row
-    msg[2:3, :] = jnp.broadcast_to(jnp.sum(target_row * target_row), (1, LANES))
+    b_norm = jnp.sum(target_row * target_row)
 
     def bytes_of(ref, sem):
         return pltpu.make_async_copy(ref, ref, sem)
@@ -235,7 +267,8 @@
     dp_rest, mp_rest = pl.ds(0, (ND - 1) * ROWS), pl.ds(0, (NM - 1) * ROWS)
     bytes_of(t_m.at[dp_rest], t_rs.at[0]).wait()
     bytes_of(t_g.at[mp_rest], t_rs.at[1]).wait()
-    msg[1:2, :] = block_row(t_g, t_m)
+    place = ((mp + 1) % NM) * ND + dp
+    msg[1:2, :] = jnp.where(iota((1, LANES), 1) == place, b_norm, block_row(t_g, t_m))
     bytes_of(b_g.at[mp_rest], b_rs).wait()
     msg[0:1, :] = block_row(b_g, t_m)
 
@@ -254,10 +287,13 @@
         rows = pl.ds(d * NM, NM)
         c_mat[rows, :] = swap_blocks(fin[rows, 0, :])
         k_mat[pl.ds(d, NM, stride=ND), :] = swap_blocks(fin[rows, 1, :])
-    norm = fin[:, 2, :][:, :1]
-
-    gram = k_mat[...]
     lane, sub = iota((NDEV, LANES), 1), iota((NDEV, LANES), 0)
+    sent = k_mat[...]
+    taken = sub == (lane + ND) % LANES
+    norm_row = jnp.sum(jnp.where(taken, sent, 0.0), axis=0, keepdims=True)
+    norm = jnp.sum(jnp.where(lane == (sub % NM) * ND + sub // NM, norm_row, 0.0), axis=1, keepdims=True)
+    mirror = jnp.sum(jnp.where(lane == sub, pltpu.roll(sent, LANES - ND, 1), 0.0), axis=0, keepdims=True)
+    gram = jnp.where(taken, mirror, sent)
     trace = jnp.sum(jnp.where(lane == sub, gram, 0.0), keepdims=True)
     damping = trace * (0.1 / (NDEV * RANK * RANK))
     inv = 1.0 / NDEV
@@ -311,14 +347,14 @@
             vmem((ND * ROWS, LANES), F32),
             vmem((NM * ROWS, LANES), F32),
             vmem((NM * ROWS, LANES), F32),
-            vmem((3, LANES), F32),
-            vmem((NDEV, 3, LANES), F32),
+            vmem((2, LANES), F32),
+            vmem((NDEV, 2, LANES), F32),
             vmem((NDEV, LANES), F32),
             vmem((NDEV, LANES), F32),
             dma((2 * PAIRS, 2)),
             dma((2,)),
             dma,
-            dma((PAIRS,)),
+            dma((PAIRS + 1,)),
             dma,
             dma((12,)),
             dma((2,)),

time: 34.7 us -> 33.4 us (0.963)
  Pallas kernels: 34 us -> 32.8 us
    pallas_call x1, Pallas kernels: 34 us -> 32.8 us  [local(): pl.pallas_call(kernel, out_shape=jax.ShapeDtypeStruct((8, NDEV), F32), in...]
where the time goes in v3:
time: 33.4 us; the launch traced here: 33.3 us
  Pallas kernels  32.8 us (98%)
  other arithmetic  0.53 us (2%)
    pallas_call x1, Pallas kernels, local(): pl.pallas_call(kernel, out_shape=jax.ShapeDtypeStruct((8, NDEV), F32), in...  32.8 us

profile of v3, /device:TPU:1, one launch (start us, length us, event | category | flops | bytes accessed | tf_op | source)
XLA Modules:
  0.0 33.3 jit_solution(3351876914931118295)
XLA Ops:
  0.0 32.8 %shard_map.64 = f32[8,128]{1,0:T(8,128)S(1)} custom-call(bf16[8,1376,256]{2,1,0:T(8,128)(2,1)} %bitcast.3, bf16[8,256,512]{2,1,0:T(8,128)(2,1)} %train_go.1, bf16[8,1376,256]{2,1,0:T(8,128)(2,1)} %bitcast.4, bf16[8,256,512]{2,1,0:T(8,128)(2,1)} %target_go.1, bf16[64,1376]{1,0:T(8,128)(2,1)} %proj_in.1, bf16[64,512]{1,0:T(8,128)(2,1)} %proj_out.1), custom_call_target="tpu_custom_call" | custom-call | tf_op jit(solution)/shard_map/pallas_call | solution.py:332
  32.8 0.5 %reduce_sum.9 = f32[128]{0:T(128)} reduce(f32[8,128]{1,0:T(8,128)S(1)} %shard_map.64, f32[]{:T(128)} %constant.0.clone.1), dimensions={0}, to_apply=%region_0.0 | reduce | flops 896 | bytes 4612 | tf_op jit(solution)/shard_map/reduce_sum | solution.py:373

commit v4 on v3

--- a/solution.py
+++ b/solution.py
@@ -18,7 +18,8 @@
 PAIRS = 8
 AHEAD = 6
 LAG = 2
-FORWARD_AT = 5
+SPLIT = 2
+FORWARD_AT = 6
 ORDER = ((0, 2), (1, 2), (0, 1), (0, 3), (1, 1), (1, 3), (0, 0), (1, 0))
 PHASE_BITS = sum(ph << q for q, (ph, _) in enumerate(ORDER))
 CHIP_BITS = sum(k << 2 * q for q, (_, k) in enumerate(ORDER))
@@ -27,6 +28,13 @@
 
 def iota(shape, axis):
     return lax.broadcasted_iota(jnp.int32, shape, axis)
+
+
+def thirds(value):
+    first = value.astype(BF16)
+    left = value - first.astype(F32)
+    second = left.astype(BF16)
+    return first, second, (left - second.astype(F32)).astype(BF16)
 
 
 def block_row(rows_ref, tile_ref):
@@ -94,12 +102,13 @@
                 copy.start()
 
     w_copies = (pltpu.make_async_copy(proj_out, w_out, w_sem.at[0]), pltpu.make_async_copy(proj_in, w_in, w_sem.at[1]))
-    first = [item_copies(s, train_in, train_go) for s in range(2)]
+    sources = ((train_in, train_go), (target_in, target_go))
+    first = [item_copies(s, *sources[ORDER[s // 2][0]]) for s in range(2 * SPLIT)]
     w_copies[0].start()
     for copies in first:
         copies[1].start()
     w_copies[1].start()
-    for copies in first:
+    for copies in first[:2]:
         copies[0].start()
 
     bar = pltpu.get_barrier_semaphore()
@@ -109,25 +118,23 @@
         pl.semaphore_signal(bar, inc=1, device_id=(y * NX + (x + o) % NX, mp), device_id_type=MESH)
         pl.semaphore_signal(bar, inc=1, device_id=(((y + o) % 4) * NX + x, mp), device_id_type=MESH)
 
-    def project_out(s):
-        item_copies(s, train_in, train_go)[1].wait()
-        part[s, :RANK, :] = lax.dot_general(w_out[...], xgo[s], (((1,), (1,)), ((), ())), preferred_element_type=F32)
-
-    def project_in(s):
-        item_copies(s, train_in, train_go)[0].wait()
-        part[s, RANK:, :] = jnp.dot(w_in[...], xin[s], preferred_element_type=F32)
-
-    def project(s):
-        for copy in item_copies(s, train_in, train_go):
-            copy.wait()
-        part[s, :RANK, :] = lax.dot_general(w_out[...], xgo[s], (((1,), (1,)), ((), ())), preferred_element_type=F32)
-        part[s, RANK:, :] = jnp.dot(w_in[...], xin[s], preferred_element_type=F32)
+    def project_out(items):
+        for s in items:
+            item_copies(s, train_in, train_go)[1].wait()
+        for s in items:
+            part[s, :RANK, :] = lax.dot_general(w_out[...], xgo[s], (((1,), (1,)), ((), ())), preferred_element_type=F32)
+
+    def project_in(items):
+        for s in items:
+            item_copies(s, train_in, train_go)[0].wait()
+        for s in items:
+            part[s, RANK:, :] = jnp.dot(w_in[...], xin[s], preferred_element_type=F32)
 
     low, high = pl.ds(0, RANK), pl.ds(RANK, RANK)
 
-    def sib_half(half, sem):
-        return pltpu.make_async_remote_copy(
-            src_ref=part.at[0, half], dst_ref=sibr.at[0, half], send_sem=sib_ss, recv_sem=sib_rs.at[sem],
+    def sib_half(q, half, sem):
+        return pltpu.make_async_remote_copy(
+            src_ref=part.at[2 * q, half], dst_ref=sibr.at[q, half], send_sem=sib_ss, recv_sem=sib_rs.at[sem],
             device_id=(dp, z * 2 + (1 - c)), device_id_type=MESH,
         )
 
@@ -155,7 +162,7 @@
         sib_copy(q).wait_recv()
         s = 2 * q + 1
         part[s] = part[s] + sibr[q]
-        for j, (ph, k) in list(enumerate(ORDER))[1:]:
+        for j, (ph, k) in list(enumerate(ORDER))[SPLIT:]:
 
             @pl.when(q == j)
             def _():
@@ -188,36 +195,45 @@
         return gradient(top, bottom)
 
     w_copies[0].wait()
-    project_out(0)
-    project_out(1)
-    for s in range(2, AHEAD):
+    project_out(range(2 * SPLIT))
+    for copies in first[2:]:
+        copies[0].start()
+    for s in range(2 * SPLIT, AHEAD):
         start_item(s)
     pl.semaphore_wait(bar, NM - 1 + 6)
-    sib_half(low, 0).start()
+    for q in range(SPLIT):
+        sib_half(q, low, q).start()
     for o in range(1, 4):
         pl.semaphore_signal(xsem, inc=1, device_id=(y * NX + (x + o) % NX, mp), device_id_type=MESH)
     w_copies[1].wait()
-    project_in(0)
-    sib_half(high, PAIRS).start()
-    project_in(1)
-    for s in range(AHEAD, AHEAD + 2):
-        start_item(s)
-    sib_half(low, 0).wait_recv()
-    part[1, :RANK, :] = part[1, :RANK, :] + sibr[0, :RANK, :]
-    ring_copy(part.at[1, low], 0, R1, zp).start()
+    for q in range(SPLIT):
+        project_in((2 * q, 2 * q + 1))
+        sib_half(q, high, PAIRS + q).start()
+        for s in range(2 * q + AHEAD, 2 * q + 2 + AHEAD):
+            start_item(s)
+        if q == 0:
+            for p in range(SPLIT):
+                sib_half(p, low, p).wait_recv()
+                part[2 * p + 1, :RANK, :] = part[2 * p + 1, :RANK, :] + sibr[p, :RANK, :]
+                ring_copy(part.at[2 * p + 1, low], ORDER[p][0], R1, zp).start()
+
+    def merge_high(p):
+        sib_half(p, high, PAIRS + p).wait_recv()
+        part[2 * p + 1, RANK:, :] = part[2 * p + 1, RANK:, :] + sibr[p, RANK:, :]
+        ring_copy(part.at[2 * p + 1, high], ORDER[p][0], R2, zm).start()
+
+    merge_high(0)
 
     def pair(q, carry):
         project_pair(q)
         sib_copy(q).start()
         start_item(2 * q + AHEAD)
         start_item(2 * q + 1 + AHEAD)
-        @pl.when(q == 1)
+        @pl.when(q == SPLIT)
         def _():
-            sib_half(high, PAIRS).wait_recv()
-            part[1, RANK:, :] = part[1, RANK:, :] + sibr[0, RANK:, :]
-            ring_copy(part.at[1, high], 0, R2, zm).start()
-
-        @pl.when(q > LAG)
+            merge_high(1)
+
+        @pl.when(q >= SPLIT + LAG)
         def _():
             merge(q - LAG)
 
@@ -227,7 +243,7 @@
 
         return carry
 
-    lax.fori_loop(1, PAIRS, pair, 0)
+    lax.fori_loop(SPLIT, PAIRS, pair, 0)
     for q in range(PAIRS - LAG, PAIRS):
         merge(q)
     forward(1)
@@ -237,6 +253,12 @@
     def mp_copy(o, src, dst, ss, rs):
         return pltpu.make_async_remote_copy(
             src_ref=src, dst_ref=dst.at[own_m], send_sem=ss, recv_sem=rs, device_id=(dp, (mp + o) % NM), device_id_type=MESH
+        )
+
+    def to_sibling(src, rows):
+        return pltpu.make_async_remote_copy(
+            src_ref=src, dst_ref=t_g.at[rows], send_sem=t_ss.at[1], recv_sem=t_rs.at[2],
+            device_id=(dp, z * 2 + (1 - c)), device_id_type=MESH,
         )
 
     def dp_copy(o, src, dst, ss, rs):
@@ -249,8 +271,9 @@
     pl.semaphore_wait(xsem, 3)
     for o in range(1, ND):
         dp_copy(o, t_own, t_m, t_ss.at[0], t_rs.at[0]).start()
-    for o in range(1, NM):
-        mp_copy(o, t_own, t_g, t_ss.at[1], t_rs.at[1]).start()
+    for dz in range(1, NZ):
+        mp_copy(2 * dz, t_own, t_g, t_ss.at[1], t_rs.at[1]).start()
+    to_sibling(t_own, own_m).start()
     t_m[own_d, :] = train_row
     t_g[own_m, :] = train_row
 
@@ -265,8 +288,12 @@
         return pltpu.make_async_copy(ref, ref, sem)
 
     dp_rest, mp_rest = pl.ds(0, (ND - 1) * ROWS), pl.ds(0, (NM - 1) * ROWS)
+    bytes_of(t_g.at[pl.ds(0, (NZ - 1) * ROWS)], t_rs.at[1]).wait()
+    for dz in range(1, NZ):
+        rows = pl.ds(pl.multiple_of((((z + dz) % NZ) * 2 + c) * ROWS, ROWS), ROWS)
+        to_sibling(t_g.at[rows], rows).start()
     bytes_of(t_m.at[dp_rest], t_rs.at[0]).wait()
-    bytes_of(t_g.at[mp_rest], t_rs.at[1]).wait()
+    bytes_of(t_g.at[pl.ds(0, NZ * ROWS)], t_rs.at[2]).wait()
     place = ((mp + 1) % NM) * ND + dp
     msg[1:2, :] = jnp.where(iota((1, LANES), 1) == place, b_norm, block_row(t_g, t_m))
     bytes_of(b_g.at[mp_rest], b_rs).wait()
@@ -276,7 +303,7 @@
 
     to_dps = [((y + dy) % 4) * NX + (x + dx) % NX for dy in (2, 1, 3, 0) for dx in (2, 1, 3, 0)]
     to_mps = [((z + dz) % NZ) * 2 + (c + dc) % 2 for dz in (2, 1, 3, 0) for dc in (1, 0)]
-    for to in [(to_dp, to_mp) for to_dp in to_dps for to_mp in to_mps][:-1]:
+    for to in [(to_dp, to_mp) for to_mp in to_mps for to_dp in to_dps][:-1]:
         pltpu.make_async_remote_copy(
             src_ref=msg, dst_ref=fin.at[me], send_sem=f_ss, recv_sem=f_rs, device_id=to, device_id_type=MESH
         ).start()
@@ -284,29 +311,36 @@
     bytes_of(fin.at[pl.ds(0, NDEV - 1)], f_rs).wait()
 
     for d in range(ND):
-        rows = pl.ds(d * NM, NM)
-        c_mat[rows, :] = swap_blocks(fin[rows, 0, :])
-        k_mat[pl.ds(d, NM, stride=ND), :] = swap_blocks(fin[rows, 1, :])
+        rows, spaced = pl.ds(d * NM, NM), pl.ds(d, NM, stride=ND)
+        c_mat[spaced, :] = swap_blocks(fin[rows, 0, :])
+        k_mat[spaced, :] = swap_blocks(fin[rows, 1, :])
     lane, sub = iota((NDEV, LANES), 1), iota((NDEV, LANES), 0)
     sent = k_mat[...]
     taken = sub == (lane + ND) % LANES
-    norm_row = jnp.sum(jnp.where(taken, sent, 0.0), axis=0, keepdims=True)
-    norm = jnp.sum(jnp.where(lane == (sub % NM) * ND + sub // NM, norm_row, 0.0), axis=1, keepdims=True)
+    norm = jnp.sum(jnp.where(taken, sent, 0.0), axis=0, keepdims=True)
     mirror = jnp.sum(jnp.where(lane == sub, pltpu.roll(sent, LANES - ND, 1), 0.0), axis=0, keepdims=True)
     gram = jnp.where(taken, mirror, sent)
-    trace = jnp.sum(jnp.where(lane == sub, gram, 0.0), keepdims=True)
-    damping = trace * (0.1 / (NDEV * RANK * RANK))
+    trace = jnp.sum(jnp.where(lane == sub, gram, 0.0), axis=0, keepdims=True)
+    damping = jnp.sum(trace, axis=1, keepdims=True) * (0.1 / (NDEV * RANK * RANK))
     inv = 1.0 / NDEV
-    u_res = c_mat[...]
+    g_first, g_second, g_third = thirds(gram)
+    gram_leading = jnp.concatenate(
+        [jnp.concatenate([g_first, g_first], axis=1), jnp.concatenate([g_second, g_second], axis=1)], axis=0
+    )
+    gram_rest = jnp.concatenate([g_third, g_first], axis=1)
+    u_res = c_mat[...].T
     u_dir, scores, dir_norm = u_res, jnp.zeros_like(u_res), norm
     for step in range(ITERS):
-        u_norm = jnp.sum(u_dir * u_dir, axis=1, keepdims=True)
+        u_norm = jnp.sum(u_dir * u_dir, axis=0, keepdims=True)
         alpha = norm / (damping * dir_norm + u_norm * inv)
         scores = scores + alpha * u_dir
         if step == ITERS - 1:
             break
-        image = lax.dot_general(u_dir, gram, (((1,), (0,)), ((), ())), precision=lax.Precision.HIGHEST, preferred_element_type=F32)
-        u_gram = jnp.sum(u_dir * image, axis=1, keepdims=True)
+        u_first, u_second, u_third = thirds(u_dir)
+        leading = jnp.dot(gram_leading, jnp.concatenate([u_first, u_second], axis=0), preferred_element_type=F32)
+        rest = jnp.dot(gram_rest, jnp.concatenate([u_first, u_third], axis=0), preferred_element_type=F32)
+        image = (rest + leading[NDEV:, :]) + leading[:NDEV, :]
+        u_gram = jnp.sum(u_dir * image, axis=0, keepdims=True)
         squared = damping * damping * dir_norm + 2.0 * inv * damping * u_norm + inv * inv * u_gram
         following = alpha * alpha * squared - norm
         u_res = u_res - alpha * (damping * u_dir + inv * image)
@@ -314,8 +348,9 @@
         u_dir = u_res + ratio * u_dir
         dir_norm = following + ratio * ratio * dir_norm
         norm = following
-    column = jnp.sum(jnp.where(lane == mp * ND + dp, scores, 0.0), axis=1, keepdims=True)
-    spread = jnp.where(lane == sub, column, 0.0)
+    row = jnp.sum(jnp.where(sub == mp * ND + dp, scores, 0.0), axis=0, keepdims=True)
+    column = jnp.sum(jnp.where(lane == sub, row, 0.0), axis=1, keepdims=True)
+    spread = jnp.where(lane == (sub % ND) * NM + sub // ND, column, 0.0)
     out_ref[...] = sum(spread[8 * d : 8 * d + 8, :] for d in range(ND))
 
     bytes_of(part.at[pl.ds(0, PAIRS)], sib_ss).wait()
@@ -354,11 +389,11 @@
             dma((2 * PAIRS, 2)),
             dma((2,)),
             dma,
-            dma((PAIRS + 1,)),
+            dma((PAIRS + SPLIT,)),
             dma,
             dma((12,)),
             dma((2,)),
-            dma((2,)),
+            dma((3,)),
             dma,
             dma,
             dma,

time: 33.4 us -> 33.1 us (level)
  Pallas kernels: 32.8 us -> 32.4 us
    pallas_call x1, Pallas kernels: 32.8 us -> 32.4 us  [local(): pl.pallas_call(kernel, out_shape=jax.ShapeDtypeStruct((8, NDEV), F32), in...]
where the time goes in v4:
time: 33.1 us; the launch traced here: 32.9 us
  Pallas kernels  32.4 us (98%)
  other arithmetic  0.53 us (2%)
    pallas_call x1, Pallas kernels, local(): pl.pallas_call(kernel, out_shape=jax.ShapeDtypeStruct((8, NDEV), F32), in...  32.4 us

profile of v4, /device:TPU:1, one launch (start us, length us, event | category | flops | bytes accessed | tf_op | source)
XLA Modules:
  0.0 32.9 jit_solution(1947136017088231218)
XLA Ops:
  0.0 32.4 %shard_map.64 = f32[8,128]{1,0:T(8,128)S(1)} custom-call(bf16[8,1376,256]{2,1,0:T(8,128)(2,1)} %bitcast.3, bf16[8,256,512]{2,1,0:T(8,128)(2,1)} %train_go.1, bf16[8,1376,256]{2,1,0:T(8,128)(2,1)} %bitcast.4, bf16[8,256,512]{2,1,0:T(8,128)(2,1)} %target_go.1, bf16[64,1376]{1,0:T(8,128)(2,1)} %proj_in.1, bf16[64,512]{1,0:T(8,128)(2,1)} %proj_out.1), custom_call_target="tpu_custom_call" | custom-call | tf_op jit(solution)/shard_map/pallas_call | solution.py:367
  32.4 0.5 %reduce_sum.9 = f32[128]{0:T(128)} reduce(f32[8,128]{1,0:T(8,128)S(1)} %shard_map.64, f32[]{:T(128)} %constant.0.clone.1), dimensions={0}, to_apply=%region_0.0 | reduce | flops 896 | bytes 4612 | tf_op jit(solution)/shard_map/reduce_sum | solution.py:408

commit v5 on v4

--- a/solution.py
+++ b/solution.py
@@ -47,7 +47,7 @@
                 new.append(acc[e * 2 + t] + tiles[t] * row)
         return tuple(new)
 
-    acc = lax.fori_loop(0, ROWS, body, tuple(jnp.zeros((8, LANES), F32) for _ in range(2 * NM)), unroll=4)
+    acc = lax.fori_loop(0, ROWS, body, tuple(jnp.zeros((8, LANES), F32) for _ in range(2 * NM)), unroll=8)
     lane, sub = iota((8, LANES), 1), iota((8, LANES), 0)
     spread = jnp.zeros((8, LANES), F32)
     for i in range(2 * NM):
@@ -269,11 +269,11 @@
     train_row = finish(0)
     t_own[...] = train_row
     pl.semaphore_wait(xsem, 3)
-    for o in range(1, ND):
-        dp_copy(o, t_own, t_m, t_ss.at[0], t_rs.at[0]).start()
     for dz in range(1, NZ):
         mp_copy(2 * dz, t_own, t_g, t_ss.at[1], t_rs.at[1]).start()
     to_sibling(t_own, own_m).start()
+    for o in range(1, ND):
+        dp_copy(o, t_own, t_m, t_ss.at[0], t_rs.at[0]).start()
     t_m[own_d, :] = train_row
     t_g[own_m, :] = train_row
 

time: 33.1 us -> 33 us (level)
  no operation moved by 1% of the time
where the time goes in v5:
time: 33 us; the launch traced here: 32.8 us
  Pallas kernels  32.3 us (98%)
  other arithmetic  0.53 us (2%)
    pallas_call x1, Pallas kernels, local(): pl.pallas_call(kernel, out_shape=jax.ShapeDtypeStruct((8, NDEV), F32), in...  32.3 us

profile of v5, /device:TPU:1, one launch (start us, length us, event | category | flops | bytes accessed | tf_op | source)
XLA Modules:
  0.0 32.8 jit_solution(10235957243128115012)
XLA Ops:
  0.0 32.3 %shard_map.64 = f32[8,128]{1,0:T(8,128)S(1)} custom-call(bf16[8,1376,256]{2,1,0:T(8,128)(2,1)} %bitcast.3, bf16[8,256,512]{2,1,0:T(8,128)(2,1)} %train_go.1, bf16[8,1376,256]{2,1,0:T(8,128)(2,1)} %bitcast.4, bf16[8,256,512]{2,1,0:T(8,128)(2,1)} %target_go.1, bf16[64,1376]{1,0:T(8,128)(2,1)} %proj_in.1, bf16[64,512]{1,0:T(8,128)(2,1)} %proj_out.1), custom_call_target="tpu_custom_call" | custom-call | tf_op jit(solution)/shard_map/pallas_call | solution.py:367
  32.3 0.5 %reduce_sum.9 = f32[128]{0:T(128)} reduce(f32[8,128]{1,0:T(8,128)S(1)} %shard_map.64, f32[]{:T(128)} %constant.0.clone.1), dimensions={0}, to_apply=%region_0.0 | reduce | flops 896 | bytes 4612 | tf_op jit(solution)/shard_map/reduce_sum | solution.py:408
